TPU v7x, 32 devices: a whole 2x2x4 slice. The times are simulated.
32 devices in a mesh: dp: 8 (over z, x), tensor: 4 (over y, core).
Axes of the slice: x: 2, y: 2, z: 4, core: 2. Of those that a mesh axis runs over, the one named last changes fastest.
Arguments:
- tokens: bfloat16 [32768, 768], P(('dp', 'tensor')), may hold values from -6 to 6
- lengths: int32 [64], P(('dp', 'tensor')), may hold values from 16 to 512, as said below
- frozen_attention_weights: bfloat16 [2, 3072, 768], P(None, ('dp', 'tensor')), may hold values from -6 to 6
- adapter_down_weights: bfloat16 [2, 2, 768, 8], replicated, may hold values from -0.21875 to 0.21875
- adapter_up_weights: bfloat16 [2, 2, 8, 768], replicated, may hold values from -1 to 1
- frozen_expand_weight: bfloat16 [2, 768, 3072], P(None, None, 'tensor'), may hold values from -0.21875 to 0.21875
- frozen_project_weight: bfloat16 [2, 3072, 768], P(None, 'tensor'), may hold values from -0.109375 to 0.109375
- frozen_norm_gains: float32 [2, 2, 768], replicated, may hold values from 0.5 to 1.5
- cotangent: bfloat16 [32768, 768], P(('dp', 'tensor')), may hold values from -6 to 6
Outputs:
- hidden_out: bfloat16 [32768, 768], P(('dp', 'tensor'))
- input_grad: float32 [32768, 768], P(('dp', 'tensor'))
- lora_a_grad: float32 [2, 2, 768, 8], replicated
- lora_b_grad: float32 [2, 2, 8, 768], replicated
Inputs may be any that keep to these rules, and one draw needn't show every extreme that they name: The first lengths[r] tokens of row r are valid, the rest are padding for keys.
All inputs are finite; a program needn't handle non-finite values.
Results may differ from a plain program's by a relative error of at most 0.033.
Values may be sent and summed in bfloat16 or wider, within the bound.
A program may use at most 256 MiB of HBM per device.

v0:
```python
import jax
import jax.numpy as jnp
from jax import lax
from jax.sharding import PartitionSpec as P

MODEL_WIDTH = 768
HEADS = 12
HEAD_DIM = 64
SEQ = 512
LAYER_COUNT = 2


epsilon = 1e-05
adapter_scale = 2.0
masked_score = -1000000000.0


def matrix_product(left_side, right_side):
    return jnp.dot(left_side, right_side, preferred_element_type=jnp.float32)


def transposed_product(left_side, right_side):
    return lax.dot_general(
        left_side, right_side, (((1,), (1,)), ((), ())), preferred_element_type=jnp.float32
    )


def leading_product(left_side, right_side):
    return lax.dot_general(
        left_side, right_side, (((0,), (0,)), ((), ())), preferred_element_type=jnp.float32
    )


def layer_norm(values, norm_gain):
    centre = jnp.mean(values, axis=-1, keepdims=True)
    centred = values - centre
    spread = jnp.mean(centred * centred, axis=-1, keepdims=True)
    return centred * lax.rsqrt(spread + epsilon) * norm_gain


def gelu_exact(values):
    return jax.nn.gelu(values, approximate=False)


def split_heads(values):
    return values.reshape(SEQ, HEADS, HEAD_DIM)


def masked_scores(query_rows, key_rows, row_length):
    scores = jnp.einsum(
        "qhd,khd->hqk",
        split_heads(query_rows),
        split_heads(key_rows),
        preferred_element_type=jnp.float32,
    ) * HEAD_DIM ** (-0.5)
    is_valid = jnp.arange(SEQ) < row_length
    return jnp.where(is_valid[None, None, :], scores, masked_score)


def attend_row(inputs):
    query_rows, key_rows, value_outputs, row_length = inputs
    scores = masked_scores(query_rows, key_rows, row_length)
    row_top = jnp.max(scores, axis=-1, keepdims=True)
    weights = jnp.exp(scores - row_top)
    row_total = jnp.sum(weights, axis=-1, keepdims=True)
    row_probs = (weights / row_total).astype(jnp.bfloat16)
    mixed_out = jnp.einsum(
        "hqk,khd->qhd", row_probs, split_heads(value_outputs), preferred_element_type=jnp.float32
    )
    return (
        mixed_out.reshape(SEQ, MODEL_WIDTH).astype(jnp.bfloat16),
        (row_top + jnp.log(row_total))[:, :, 0],
    )


def attend_back(inputs):
    query_rows, key_rows, value_outputs, grad_mixed, log_totals, row_length = inputs
    scores = masked_scores(query_rows, key_rows, row_length)
    row_probs = jnp.exp(scores - log_totals[:, :, None])
    grad_heads = split_heads(grad_mixed)
    grad_probs = jnp.einsum(
        "qhd,khd->hqk", grad_heads, split_heads(value_outputs), preferred_element_type=jnp.float32
    )
    value_gradient = jnp.einsum(
        "hqk,qhd->khd",
        row_probs.astype(jnp.bfloat16),
        grad_heads,
        preferred_element_type=jnp.float32,
    )
    grad_scores = (
        row_probs * (grad_probs - jnp.sum(grad_probs * row_probs, axis=-1, keepdims=True))
    ).astype(jnp.bfloat16)
    score_scale = HEAD_DIM ** (-0.5)
    query_gradient = (
        jnp.einsum(
            "hqk,khd->qhd", grad_scores, split_heads(key_rows), preferred_element_type=jnp.float32
        )
        * score_scale
    )
    grad_keys = (
        jnp.einsum(
            "hqk,qhd->khd", grad_scores, split_heads(query_rows), preferred_element_type=jnp.float32
        )
        * score_scale
    )
    return (
        query_gradient.reshape(SEQ, MODEL_WIDTH).astype(jnp.bfloat16),
        grad_keys.reshape(SEQ, MODEL_WIDTH).astype(jnp.bfloat16),
        value_gradient.reshape(SEQ, MODEL_WIDTH).astype(jnp.bfloat16),
    )


def ffn_back(grad_rows, pre_rows, first_weight, second_weight):
    grad_act = transposed_product(grad_rows, second_weight)
    gelu_out, gelu_pull = jax.vjp(gelu_exact, pre_rows)
    grad_pre = gelu_pull(grad_act)[0].astype(jnp.bfloat16)
    return transposed_product(grad_pre, first_weight)


def local(
    tokens,
    lengths,
    frozen_attention_weights,
    adapter_down_weights,
    adapter_up_weights,
    frozen_expand_weight,
    frozen_project_weight,
    frozen_norm_gains,
    cotangent,
):
    local_tokens = tokens.shape[0]
    local_rows = lengths.shape[0]
    second_inputs = tokens
    saved_layers = []
    for layer_position in range(LAYER_COUNT):
        frozen = lax.all_gather(
            frozen_attention_weights[layer_position], ("dp", "tensor"), axis=0, tiled=True
        )
        query_matrix = frozen[0:MODEL_WIDTH]
        key_weight = frozen[MODEL_WIDTH : 2 * MODEL_WIDTH]
        value_matrix = frozen[2 * MODEL_WIDTH : 3 * MODEL_WIDTH]
        output_weight = frozen[3 * MODEL_WIDTH : 4 * MODEL_WIDTH]
        reduced_query = matrix_product(
            second_inputs, adapter_down_weights[layer_position, 0]
        ).astype(jnp.bfloat16)
        reduced_values = matrix_product(
            second_inputs, adapter_down_weights[layer_position, 1]
        ).astype(jnp.bfloat16)
        query_rows = (
            matrix_product(second_inputs, query_matrix)
            + adapter_scale * matrix_product(reduced_query, adapter_up_weights[layer_position, 0])
        ).astype(jnp.bfloat16)
        key_rows = matrix_product(second_inputs, key_weight).astype(jnp.bfloat16)
        value_outputs = (
            matrix_product(second_inputs, value_matrix)
            + adapter_scale * matrix_product(reduced_values, adapter_up_weights[layer_position, 1])
        ).astype(jnp.bfloat16)
        mixed_out, log_totals = lax.map(
            attend_row,
            (
                query_rows.reshape(local_rows, SEQ, MODEL_WIDTH),
                key_rows.reshape(local_rows, SEQ, MODEL_WIDTH),
                value_outputs.reshape(local_rows, SEQ, MODEL_WIDTH),
                lengths,
            ),
        )
        mixed_out = mixed_out.reshape(local_tokens, MODEL_WIDTH)
        pre_first = second_inputs.astype(jnp.float32) + matrix_product(mixed_out, output_weight)
        normed = layer_norm(pre_first, frozen_norm_gains[layer_position, 0]).astype(jnp.bfloat16)
        first_weight, second_weight = (
            lax.all_gather(frozen_expand_weight[layer_position], "tensor", axis=1, tiled=True),
            lax.all_gather(frozen_project_weight[layer_position], "tensor", axis=0, tiled=True),
        )
        hidden_pre = matrix_product(normed, first_weight)
        ffn_result = matrix_product(gelu_exact(hidden_pre).astype(jnp.bfloat16), second_weight)
        pre_second = normed.astype(jnp.float32) + ffn_result
        output = layer_norm(pre_second, frozen_norm_gains[layer_position, 1])
        saved_layers.append(
            (
                second_inputs,
                reduced_query,
                reduced_values,
                query_rows,
                key_rows,
                value_outputs,
                log_totals,
                pre_first,
                pre_second,
                hidden_pre,
                first_weight,
                second_weight,
            )
        )
        second_inputs = output.astype(jnp.bfloat16)
    grad_out = cotangent.astype(jnp.float32)
    grads_a = [None] * LAYER_COUNT
    grads_b = [None] * LAYER_COUNT
    for layer_position in reversed(range(LAYER_COUNT)):
        (
            layer_in,
            reduced_query,
            reduced_values,
            query_rows,
            key_rows,
            value_outputs,
            log_totals,
            pre_first,
            pre_second,
            hidden_pre,
            first_weight,
            second_weight,
        ) = saved_layers[layer_position]
        frozen = lax.all_gather(
            frozen_attention_weights[layer_position], ("dp", "tensor"), axis=0, tiled=True
        )
        query_matrix = frozen[0:MODEL_WIDTH]
        key_weight = frozen[MODEL_WIDTH : 2 * MODEL_WIDTH]
        value_matrix = frozen[2 * MODEL_WIDTH : 3 * MODEL_WIDTH]
        output_weight = frozen[3 * MODEL_WIDTH : 4 * MODEL_WIDTH]
        second_gain = frozen_norm_gains[layer_position, 1]
        first_gain = frozen_norm_gains[layer_position, 0]
        norm_out, pull_second = jax.vjp(lambda values: layer_norm(values, second_gain), pre_second)
        grad_second = pull_second(grad_out)[0]
        grad_ffn = grad_second.astype(jnp.bfloat16)
        grad_normed = ffn_back(grad_ffn, hidden_pre, first_weight, second_weight)
        grad_normed = grad_second + grad_normed
        norm_first, pull_first = jax.vjp(lambda values: layer_norm(values, first_gain), pre_first)
        grad_first = pull_first(grad_normed)[0]
        grad_mixed = transposed_product(grad_first.astype(jnp.bfloat16), output_weight).astype(
            jnp.bfloat16
        )
        query_gradient, grad_keys, value_gradient = lax.map(
            attend_back,
            (
                query_rows.reshape(local_rows, SEQ, MODEL_WIDTH),
                key_rows.reshape(local_rows, SEQ, MODEL_WIDTH),
                value_outputs.reshape(local_rows, SEQ, MODEL_WIDTH),
                grad_mixed.reshape(local_rows, SEQ, MODEL_WIDTH),
                log_totals,
                lengths,
            ),
        )
        query_gradient = query_gradient.reshape(local_tokens, MODEL_WIDTH)
        grad_keys = grad_keys.reshape(local_tokens, MODEL_WIDTH)
        value_gradient = value_gradient.reshape(local_tokens, MODEL_WIDTH)
        query_adapter_gradient = (
            adapter_scale
            * transposed_product(query_gradient, adapter_up_weights[layer_position, 0])
        ).astype(jnp.bfloat16)
        value_adapter_gradient = (
            adapter_scale
            * transposed_product(value_gradient, adapter_up_weights[layer_position, 1])
        ).astype(jnp.bfloat16)
        grads_a[layer_position] = jnp.stack(
            [
                leading_product(layer_in, query_adapter_gradient),
                leading_product(layer_in, value_adapter_gradient),
            ]
        )
        grads_b[layer_position] = jnp.stack(
            [
                adapter_scale * leading_product(reduced_query, query_gradient),
                adapter_scale * leading_product(reduced_values, value_gradient),
            ]
        )
        grad_out = (
            grad_first
            + transposed_product(query_gradient, query_matrix)
            + transposed_product(grad_keys, key_weight)
            + transposed_product(value_gradient, value_matrix)
            + transposed_product(query_adapter_gradient, adapter_down_weights[layer_position, 0])
            + transposed_product(value_adapter_gradient, adapter_down_weights[layer_position, 1])
        )
    grad_a_sum, grad_b_sum = lax.psum((jnp.stack(grads_a), jnp.stack(grads_b)), ("dp", "tensor"))
    return (second_inputs, grad_out, grad_a_sum, grad_b_sum)


def solution(mesh):
    placed = (
        P(("dp", "tensor"), None),
        P(("dp", "tensor")),
        P(None, ("dp", "tensor"), None),
        P(),
        P(),
        P(None, None, "tensor"),
        P(None, "tensor", None),
        P(),
        P(("dp", "tensor"), None),
    )
    return jax.shard_map(
        local,
        mesh=mesh,
        in_specs=placed,
        out_specs=(P(("dp", "tensor"), None), P(("dp", "tensor"), None), P(), P()),
        check_vma=False,
    )
```

profile of v0, /device:TPU:0, one launch (start us, length us, event | category | flops | bytes accessed | tf_op | source)
XLA Modules:
  0.0 761.3 jit_solution(5970971028540514632)
XLA Ops:
  22.4 55.4 %all-gather.13.cloned.1.call-done = bf16[1,3072,768]{2,1,0:T(8,128)(2,1)} async-done(((bf16[1,96,768]{2,1,0:T(8,128)(2,1)}), bf16[1,3072,768]{2,1,0:T(8,128)(2,1)}) %all-gather.13.cloned.1.call-update) | async-done | bytes 4718608 | tf_op jit(solution)/shard_map/all_gather | solution.py:136
  100.0 26.4 %while.52 = (s32[]{:T(128)}, bf16[2,512,768]{2,1,0:T(8,128)(2,1)}, f32[2,12,512]{2,1,0:T(8,128)S(1)}, bf16[2,512,768]{1,2,0:T(8,128)(2,1)S(1)}, s32[2]{0:T(128)S...) while((s32[]{:T(128)}, bf16[2,512,768]{2,1,0:T(8,128)(2,1)}, ...), condition=%wide.region_3.4_spmd, body=%wide.region_0.3_spmd.sunk | while | flops 843442688 | bytes 48982640 | solution.py:158
  126.4 4.4 fusion.157
  133.5 36.2 %fusion.30 = (f32[1024,3072]{1,0:T(8,128)}, f32[1024,3072]{1,0:T(8,128)}) fusion(bf16[1,768,3072]{2,1,0:T(8,128)(2,1)} %all-gather.15.cloned.1.call-done, f32[1024,768]{0,1:T(8,128)} %copy-done.22, f32[768]{0:T(1024)S(1)} %copy-done.77, f32[1024]{0:T(1024)S(1)} %fusion.140, f32[1024]{0:T(1024)S(1)} %broadcast_multiply_fusion.3), kind=kOutput, calls=%fused_computation.72 | convolution fusion | flops 5030019072 | bytes 33041408 | tf_op jit(solution)/shard_map/dot_general | solution.py:19
  169.7 15.7 %fusion.158 = (f32[1024]{0:T(1024)S(1)}, f32[1024,768]{0,1:T(8,128)S(1)}) fusion(bf16[1,3072,768]{2,1,0:T(8,128)(2,1)} %all-gather.17.cloned.1.call-done, f32[1024,3072]{1,0:T(8,128)} %get-tuple-element.382, f32[1024,3072]{1,0:T(8,128)} %get-tuple-element.383, f32[768]{0:T(1024)S(1)} %copy-done.77, f32[1024]{0:T(1024)S(1)} %fusion.140, ...), kind=kOutput, calls=%fused_computation.285 | convolution fusion | flops 4846779392 | bytes 36191232 | tf_op jit(solution)/shard_map/dot_general | solution.py:19
  188.6 32.5 %all-gather.19.cloned.1.call-done = bf16[1,3072,768]{2,1,0:T(8,128)(2,1)} async-done(((bf16[1,96,768]{2,1,0:T(8,128)(2,1)}), bf16[1,3072,768]{2,1,0:T(8,128)(2,1)}) %all-gather.19.cloned.1.call-update) | async-done | bytes 4718608 | tf_op jit(solution)/shard_map/all_gather | solution.py:136
  243.0 28.1 %while.53 = (s32[]{:T(128)}, bf16[2,512,768]{2,1,0:T(8,128)(2,1)}, f32[2,12,512]{2,1,0:T(8,128)S(1)}, bf16[2,512,768]{1,2,0:T(8,128)(2,1)}, s32[2]{0:T(128)S(1)}...) while((s32[]{:T(128)}, bf16[2,512,768]{2,1,0:T(8,128)(2,1)}, ...), condition=%wide.region_11.12_spmd, body=%wide.region_8.11_spmd.sunk | while | flops 843442688 | bytes 48982640 | solution.py:158
  277.0 36.0 %fusion.31 = (f32[1024,3072]{1,0:T(8,128)}, f32[1024,3072]{1,0:T(8,128)}) fusion(bf16[1,768,3072]{2,1,0:T(8,128)(2,1)} %all-gather.21.cloned.1.call-done, f32[1024,768]{0,1:T(8,128)} %copy-done.23, f32[768]{0:T(1024)S(1)} %copy-done.79, f32[1024]{0:T(1024)S(1)} %fusion.142, f32[1024]{0:T(1024)S(1)} %broadcast_multiply_fusion.1), kind=kOutput, calls=%fused_computation.73 | convolution fusion | flops 5030019072 | bytes 33041408 | tf_op jit(solution)/shard_map/dot_general | solution.py:19
  313.1 16.9 %fusion.160 = (f32[1024]{0:T(1024)S(1)}, f32[1024,768]{0,1:T(8,128)}) fusion(bf16[1,3072,768]{2,1,0:T(8,128)(2,1)} %all-gather.23.cloned.1.call-done, f32[1024,3072]{1,0:T(8,128)} %get-tuple-element.388, f32[1024,3072]{1,0:T(8,128)} %get-tuple-element.389, f32[768]{0:T(1024)S(1)} %copy-done.79, f32[1024]{0:T(1024)S(1)} %fusion.142, ...), kind=kOutput, calls=%fused_computation.287 | convolution fusion | flops 4846779392 | bytes 36191232 | tf_op jit(solution)/shard_map/dot_general | solution.py:19
  335.2 22.3 %multiply_reduce_fusion.4 = (f32[1024]{0:T(1024)S(1)}, f32[1024,768]{0,1:T(8,128)}) fusion(f32[1024,768]{0,1:T(8,128)} %copy-done.23, f32[1024]{0:T(1024)S(1)} %broadcast_multiply_fusion.1, f32[768]{0:T(1024)S(1)} %copy-done.79, bf16[1,768,3072]{2,1,0:T(8,128)(2,1)} %all-gather.21.cloned.1.call-done, f32[1024,3072]{1,0:T(8,128)} %get-tuple-element.388, ...), kind=kOutput, calls=%fused_computation.131 | convolution fusion | flops 9725017088 | bytes 45643776 | tf_op jit(solution)/shard_map/dot_general | solution.py:23
  361.6 4.8 convolution_convert_fusion.1
  370.2 98.8 %while.54 = (s32[]{:T(128)}, bf16[2,512,768]{2,1,0:T(8,128)(2,1)}, bf16[2,512,768]{2,1,0:T(8,128)(2,1)}, bf16[2,512,768]{2,1,0:T(8,128)(2,1)}, bf16[2,512,768]{1...) while((s32[]{:T(128)}, bf16[2,512,768]{2,1,0:T(8,128)(2,1)}, ...), condition=%wide.region_22.23_spmd, body=%wide.region_20.22_spmd.sunk | while | flops 2062412288 | bytes 201895312 | solution.py:232
  372.2 6.4 fusion.295
  382.2 11.5 %multiply_reduce_fusion.12 = (f32[12,512]{1,0:T(8,128)S(1)}, f32[12,512,512]{1,2,0:T(8,128)}) fusion(f32[12,512,512]{1,2,0:T(8,128)} %fusion.295, f32[12,512]{1,0:T(8,128)S(1)} %dynamic-slice_bitcast_fusion.4, pred[512]{0:T(512)(128)(4,1)S(1)} %iota_compare_fusion.10, bf16[512,12,64]{0,2,1:T(8,128)(2,1)S(1)} %bitcast.420, ...), kind=kOutput, calls=%fused_computation.31.clone.1 | convolution fusion | flops 418375680 | bytes 26788352 | tf_op jit(solution)/shard_map/while/body/eval_jaxpr/qhd,khd->hqk/dot_general | solution.py:81
  394.8 7.1 multiply_convert_fusion.26
  404.8 7.5 fusion.296
  421.3 6.4 fusion.295
  431.3 11.5 %multiply_reduce_fusion.12 = (f32[12,512]{1,0:T(8,128)S(1)}, f32[12,512,512]{1,2,0:T(8,128)}) fusion(f32[12,512,512]{1,2,0:T(8,128)} %fusion.295, f32[12,512]{1,0:T(8,128)S(1)} %dynamic-slice_bitcast_fusion.4, pred[512]{0:T(512)(128)(4,1)S(1)} %iota_compare_fusion.10, bf16[512,12,64]{0,2,1:T(8,128)(2,1)S(1)} %bitcast.420, ...), kind=kOutput, calls=%fused_computation.31.clone.1 | convolution fusion | flops 418375680 | bytes 26788352 | tf_op jit(solution)/shard_map/while/body/eval_jaxpr/qhd,khd->hqk/dot_general | solution.py:81
  443.9 7.1 multiply_convert_fusion.26
  453.9 7.5 fusion.296
  486.8 21.6 %multiply_reduce_fusion.2 = (f32[1024]{0:T(1024)S(1)}, f32[1024,768]{0,1:T(8,128)}) fusion(f32[1024,768]{0,1:T(8,128)} %copy-done.22, f32[1024]{0:T(1024)S(1)} %copy-done.60, f32[768]{0:T(1024)S(1)} %copy-done.78, bf16[1,768,3072]{2,1,0:T(8,128)(2,1)} %all-gather.15.cloned.1.call-done, f32[1024,3072]{1,0:T(8,128)} %get-tuple-element.382, ...), kind=kOutput, calls=%fused_computation.127 | convolution fusion | flops 9721871360 | bytes 47213568 | tf_op jit(solution)/shard_map/dot_general | solution.py:23
  512.4 4.8 convolution_convert_fusion
  521.0 98.1 %while.55 = (s32[]{:T(128)}, bf16[2,512,768]{2,1,0:T(8,128)(2,1)}, bf16[2,512,768]{2,1,0:T(8,128)(2,1)}, bf16[2,512,768]{2,1,0:T(8,128)(2,1)}, bf16[2,512,768]{1...) while((s32[]{:T(128)}, bf16[2,512,768]{2,1,0:T(8,128)(2,1)}, ...), condition=%wide.region_29.30_spmd, body=%wide.region_27.29_spmd.sunk | while | flops 2062412288 | bytes 201501520 | solution.py:232
  523.6 6.4 fusion.307
  532.8 11.5 %multiply_reduce_fusion.13 = (f32[12,512]{1,0:T(8,128)S(1)}, f32[12,512,512]{1,2,0:T(8,128)}) fusion(f32[12,512,512]{1,2,0:T(8,128)} %fusion.307, f32[12,512]{1,0:T(8,128)S(1)} %dynamic-slice_bitcast_fusion.5, pred[512]{0:T(512)(128)(4,1)S(1)} %iota_compare_fusion.11, bf16[512,12,64]{0,2,1:T(8,128)(2,1)S(1)} %bitcast.422, ...), kind=kOutput, calls=%fused_computation.51.clone.1 | convolution fusion | flops 418375680 | bytes 26788352 | tf_op jit(solution)/shard_map/while/body/eval_jaxpr/qhd,khd->hqk/dot_general | solution.py:81
  545.4 7.1 multiply_convert_fusion.29
  555.4 7.5 fusion.308
  572.5 6.4 fusion.307
  581.7 11.5 %multiply_reduce_fusion.13 = (f32[12,512]{1,0:T(8,128)S(1)}, f32[12,512,512]{1,2,0:T(8,128)}) fusion(f32[12,512,512]{1,2,0:T(8,128)} %fusion.307, f32[12,512]{1,0:T(8,128)S(1)} %dynamic-slice_bitcast_fusion.5, pred[512]{0:T(512)(128)(4,1)S(1)} %iota_compare_fusion.11, bf16[512,12,64]{0,2,1:T(8,128)(2,1)S(1)} %bitcast.422, ...), kind=kOutput, calls=%fused_computation.51.clone.1 | convolution fusion | flops 418375680 | bytes 26788352 | tf_op jit(solution)/shard_map/while/body/eval_jaxpr/qhd,khd->hqk/dot_general | solution.py:81
  594.3 7.1 multiply_convert_fusion.29
  604.3 7.5 fusion.308
  642.7 108.4 %all-reduce.3.cloned.1.call-done = (f32[2,2,768,8]{2,3,1,0:T(8,128)}, f32[2,2,8,768]{3,2,1,0:T(8,128)}) async-done(((f32[2,2,768,8]{2,3,1,0:T(8,128)}, f32[2,2,8,768]{3,2,1,0:T(8,128)}), (f32[2,2,768,8]{2,3,1,0:T(8,128)}, f32[2,2,8,768]{3,2,1,0:T(8,128)})) %all-reduce.3.cloned.1.call-update) | async-done | bytes 196624 | tf_op jit(solution)/shard_map/psum | solution.py:274
  (425 shorter events, 254.7 us)
Async XLA Ops:
  7.2 70.6 %all-gather.13.cloned.1.call-start = ((), (), s32[]{:S(2)}) async-start(), calls=%async_computation | async-start | bytes 4866048 | tf_op jit(solution)/shard_map/all_gather | solution.py:136
  8.9 124.5 %all-gather.15.cloned.1.call-start = ((), (), s32[]{:S(2)}) async-start(), calls=%async_computation.1 | async-start | bytes 5898240 | tf_op jit(solution)/shard_map/all_gather | solution.py:171
  12.2 157.4 %all-gather.17.cloned.1.call-start = ((), (), s32[]{:S(2)}) async-start(), calls=%async_computation.2 | async-start | bytes 5898240 | tf_op jit(solution)/shard_map/all_gather | solution.py:172
  15.6 205.5 %all-gather.19.cloned.1.call-start = ((), (), s32[]{:S(2)}) async-start(), calls=%async_computation.3 | async-start | bytes 4866048 | tf_op jit(solution)/shard_map/all_gather | solution.py:136
  16.2 260.8 %all-gather.21.cloned.1.call-start = ((), (), s32[]{:S(2)}) async-start(), calls=%async_computation.4 | async-start | bytes 5898240 | tf_op jit(solution)/shard_map/all_gather | solution.py:171
  16.8 296.3 %all-gather.23.cloned.1.call-start = ((), (), s32[]{:S(2)}) async-start(), calls=%async_computation.5 | async-start | bytes 5898240 | tf_op jit(solution)/shard_map/all_gather | solution.py:172
  17.4 733.8 %all-reduce.3.cloned.1.call-start = ((), (), s32[]{:S(2)}) async-start(), calls=%async_computation.6 | async-start | bytes 393216 | tf_op jit(solution)/shard_map/psum | solution.py:274
  17.9 62.5 %copy-start.47 = (bf16[1024,8]{0,1:T(8,128)(2,1)}, bf16[1024,8]{0,1:T(8,128)(2,1)S(1)}, u32[]{:S(2)}) copy-start(bf16[1024,8]{0,1:T(8,128)(2,1)S(1)} %convolution_convert_fusion.7) | copy-start | bytes 49156
  18.5 68.9 %copy-start.45 = (bf16[1024,8]{0,1:T(8,128)(2,1)}, bf16[1024,8]{0,1:T(8,128)(2,1)S(1)}, u32[]{:S(2)}) copy-start(bf16[1024,8]{0,1:T(8,128)(2,1)S(1)} %convolution_convert_fusion.6) | copy-start | bytes 49156
  22.4 58.1 %copy-start.41 = (bf16[2,2,8,768]{3,2,1,0:T(8,128)(2,1)S(1)}, bf16[2,2,8,768]{3,2,1,0:T(8,128)(2,1)}, u32[]{:S(2)}) copy-start(bf16[2,2,8,768]{3,2,1,0:T(8,128)(2,1)} %param.21) | copy-start | bytes 147460
  130.8 38.8 %copy-start.59 = (f32[1024]{0:T(1024)}, f32[1024]{0:T(1024)S(1)}, u32[]{:S(2)}) copy-start(f32[1024]{0:T(1024)S(1)} %broadcast_multiply_fusion.3) | copy-start | bytes 12292
  133.4 36.2 %copy-start.70 = (f32[1024]{0:T(1024)}, f32[1024]{0:T(1024)S(1)}, u32[]{:S(2)}) copy-start(f32[1024]{0:T(1024)S(1)} %fusion.140) | copy-start | bytes 12292
  188.3 36.0 %copy-start.51 = (bf16[1024,8]{0,1:T(8,128)(2,1)}, bf16[1024,8]{0,1:T(8,128)(2,1)S(1)}, u32[]{:S(2)}) copy-start(bf16[1024,8]{0,1:T(8,128)(2,1)S(1)} %convolution_convert_fusion.4) | copy-start | bytes 49156
  188.6 42.2 %copy-start.49 = (bf16[1024,8]{0,1:T(8,128)(2,1)}, bf16[1024,8]{0,1:T(8,128)(2,1)S(1)}, u32[]{:S(2)}) copy-start(bf16[1024,8]{0,1:T(8,128)(2,1)S(1)} %convolution_convert_fusion.5) | copy-start | bytes 49156
  188.6 35.7 %copy-start.42 = (bf16[2,2,8,768]{3,2,1,0:T(8,128)(2,1)S(1)}, bf16[2,2,8,768]{3,2,1,0:T(8,128)(2,1)}, u32[]{:S(2)}) copy-start(bf16[2,2,8,768]{3,2,1,0:T(8,128)(2,1)} %param.21) | copy-start | bytes 147460
  313.1 17.0 %copy-start.18 = (bf16[1024,768]{0,1:T(8,128)(2,1)S(1)}, bf16[1024,768]{0,1:T(8,128)(2,1)}, u32[]{:S(2)}) copy-start(bf16[1024,768]{0,1:T(8,128)(2,1)} %copy.61) | copy-start | bytes 4718596
  313.1 17.0 %copy-start.65 = (f32[768]{0:T(1024)S(1)}, f32[768]{0:T(1024)}, u32[]{:S(2)}) copy-start(f32[768]{0:T(1024)} %get-tuple-element.276) | copy-start | bytes 9220
  370.2 98.8 %copy-start.52 = (bf16[1024,8]{0,1:T(8,128)(2,1)S(1)}, bf16[1024,8]{0,1:T(8,128)(2,1)}, u32[]{:S(2)}) copy-start(bf16[1024,8]{0,1:T(8,128)(2,1)} %copy-done.51) | copy-start | bytes 49156
  370.2 101.3 %copy-start.43 = (bf16[2,2,8,768]{3,2,1,0:T(8,128)(2,1)S(1)}, bf16[2,2,8,768]{3,2,1,0:T(8,128)(2,1)}, u32[]{:S(2)}) copy-start(bf16[2,2,8,768]{3,2,1,0:T(8,128)(2,1)} %param.21) | copy-start | bytes 147460
  382.2 11.5 %slice-start = ((s8[12582912]{0:T(1024)(128)(4,1)}), s8[4194304]{0:T(1024)(128)(4,1)S(1)}, s32[]{:S(2)}) async-start(s8[12582912]{0:T(1024)(128)(4,1)} %bitcast.406), calls=%async_computation.7 | async-start | bytes 8388608 | tf_op jit(solution)/shard_map/while
  382.2 11.5 %slice-start.1 = ((s8[12582912]{0:T(1024)(128)(4,1)}), s8[4194304]{0:T(1024)(128)(4,1)S(1)}, s32[]{:S(2)}) async-start(s8[12582912]{0:T(1024)(128)(4,1)} %bitcast.406), calls=%async_computation.8 | async-start | bytes 8388608 | tf_op jit(solution)/shard_map/while
  382.2 12.6 %slice-start.2 = ((s8[12582912]{0:T(1024)(128)(4,1)}), s8[4194304]{0:T(1024)(128)(4,1)S(1)}, s32[]{:S(2)}) async-start(s8[12582912]{0:T(1024)(128)(4,1)} %bitcast.406), calls=%async_computation.9 | async-start | bytes 8388608 | tf_op jit(solution)/shard_map/while
  431.3 11.5 %slice-start = ((s8[12582912]{0:T(1024)(128)(4,1)}), s8[4194304]{0:T(1024)(128)(4,1)S(1)}, s32[]{:S(2)}) async-start(s8[12582912]{0:T(1024)(128)(4,1)} %bitcast.406), calls=%async_computation.7 | async-start | bytes 8388608 | tf_op jit(solution)/shard_map/while
  431.3 12.6 %slice-start.2 = ((s8[12582912]{0:T(1024)(128)(4,1)}), s8[4194304]{0:T(1024)(128)(4,1)S(1)}, s32[]{:S(2)}) async-start(s8[12582912]{0:T(1024)(128)(4,1)} %bitcast.406), calls=%async_computation.9 | async-start | bytes 8388608 | tf_op jit(solution)/shard_map/while
  486.8 21.7 %copy-start.62 = (f32[1024]{0:T(1024)S(1)}, f32[1024]{0:T(1024)}, u32[]{:S(2)}) copy-start(f32[1024]{0:T(1024)} %copy-done.61) | copy-start | bytes 12292
  486.8 21.7 %copy-start.71 = (f32[1024]{0:T(1024)S(1)}, f32[1024]{0:T(1024)}, u32[]{:S(2)}) copy-start(f32[1024]{0:T(1024)} %copy-done.70) | copy-start | bytes 12292
  521.0 98.1 %copy-start.48 = (bf16[1024,8]{0,1:T(8,128)(2,1)S(1)}, bf16[1024,8]{0,1:T(8,128)(2,1)}, u32[]{:S(2)}) copy-start(bf16[1024,8]{0,1:T(8,128)(2,1)} %copy-done.47) | copy-start | bytes 49156
  521.0 100.0 %copy-start.44 = (bf16[2,2,8,768]{3,2,1,0:T(8,128)(2,1)S(1)}, bf16[2,2,8,768]{3,2,1,0:T(8,128)(2,1)}, u32[]{:S(2)}) copy-start(bf16[2,2,8,768]{3,2,1,0:T(8,128)(2,1)} %param.21) | copy-start | bytes 147460
  532.8 11.5 %slice-start.3 = ((s8[12582912]{0:T(1024)(128)(4,1)}), s8[4194304]{0:T(1024)(128)(4,1)S(1)}, s32[]{:S(2)}) async-start(s8[12582912]{0:T(1024)(128)(4,1)} %bitcast.408), calls=%async_computation.10 | async-start | bytes 8388608 | tf_op jit(solution)/shard_map/while
  532.8 12.6 %slice-start.5 = ((s8[12582912]{0:T(1024)(128)(4,1)}), s8[4194304]{0:T(1024)(128)(4,1)S(1)}, s32[]{:S(2)}) async-start(s8[12582912]{0:T(1024)(128)(4,1)} %bitcast.408), calls=%async_computation.12 | async-start | bytes 8388608 | tf_op jit(solution)/shard_map/while
  581.6 11.5 %slice-start.3 = ((s8[12582912]{0:T(1024)(128)(4,1)}), s8[4194304]{0:T(1024)(128)(4,1)S(1)}, s32[]{:S(2)}) async-start(s8[12582912]{0:T(1024)(128)(4,1)} %bitcast.408), calls=%async_computation.10 | async-start | bytes 8388608 | tf_op jit(solution)/shard_map/while
  581.7 12.6 %slice-start.5 = ((s8[12582912]{0:T(1024)(128)(4,1)}), s8[4194304]{0:T(1024)(128)(4,1)S(1)}, s32[]{:S(2)}) async-start(s8[12582912]{0:T(1024)(128)(4,1)} %bitcast.408), calls=%async_computation.12 | async-start | bytes 8388608 | tf_op jit(solution)/shard_map/while
  (81 other events, 301.8 us)
Sparse Core Ops, SparseCore 0:
  11.5 66.2 all-gather.12
  79.4 36.2 all-gather.14
  117.2 37.4 all-gather.16
  157.5 63.5 all-gather.18
  222.5 36.2 all-gather.20
  260.2 37.4 all-gather.22
  628.2 122.9 all-reduce.2
where the time goes:
time: 769 us; the launch traced here: 761 us
  matrix products  378 us (49%)
  waiting for transfers between devices  198 us (26%)
  local copies, waits for them, and re-layouts  107 us (14%)
  other arithmetic  60.7 us (8%)
  between operations  15.3 us (2%)
    dot_general x20, matrix products, matrix_product(): return jnp.dot(left_side, right_side, preferred_element_type=jnp.float32)  142 us
    psum x1, waiting for transfers between devices, local(): lax.psum((jnp.stack(grads_a), jnp.stack(grads_b)), ('dp', 'tensor'))  108 us
    all_gather x2, waiting for transfers between devices, local(): lax.all_gather(frozen_attention_weights[layer_position], ('dp', 'tensor')...  87.9 us
    dot_general x18, matrix products, transposed_product(): lax.dot_general(left_side, right_side, (((1,), (1,)), ((), ())), preferre...  76.4 us
    dot_general x4, matrix products, attend_back(): jnp.einsum('qhd,khd->hqk', grad_heads, split_heads(value_outputs), prefer...  45.8 us
    dot_general x8, matrix products, masked_scores(): jnp.einsum('qhd,khd->hqk', split_heads(query_rows), split_heads(key_rows)...  38 us
    dot_general x4, matrix products, attend_back(): jnp.einsum('hqk,qhd->khd', row_probs.astype(jnp.bfloat16), grad_heads, pr...  30.2 us
    convert_element_type x4, other arithmetic, attend_back(): grad_scores = (row_probs * (grad_probs - jnp.sum(grad_probs * row_probs,...  28.4 us
  transfers between devices with their start and end apart: 7, of which 3 were waited for; matrix products, arithmetic and copies ran while one was open for 29% of the time, Pallas kernels for 0%

commit v1 on v0

v1 whole, which is shorter than its diff:
```python
import functools
import jax
import jax.numpy as jnp
from jax import lax
from jax.experimental import pallas as pl
from jax.experimental.pallas import tpu as pltpu
from jax.sharding import PartitionSpec as P

WIDTH = 768
HEADS = 12
HEAD_DIM = 64
SEQ = 512
RANK = 8
EPS = 1e-05
BF = jnp.bfloat16
F32 = jnp.float32
VMEM_LIMIT = 60 * 1024 * 1024
EXP2_SCALE = 1.4426950408889634 * HEAD_DIM ** (-0.5)


def dot(a, b):
    return jnp.dot(a, b, preferred_element_type=F32)


def dot_nt(a, b):
    return lax.dot_general(a, b, (((1,), (1,)), ((), ())), preferred_element_type=F32)


def dot_tn(a, b):
    return lax.dot_general(a, b, (((0,), (0,)), ((), ())), preferred_element_type=F32)


def mean_rows(v):
    return jnp.sum(v, axis=-1, keepdims=True) * (1.0 / WIDTH)


def params(n):
    return pltpu.CompilerParams(
        dimension_semantics=("arbitrary",) * n, vmem_limit_bytes=VMEM_LIMIT
    )


GROUP = 4


def attend_kernel(len_ref, x_ref, w_ref, a_ref, b_ref, g_ref,
                  qkv_ref, u_ref, o_ref, e_ref, rinv_ref, n1_ref, r1_ref, bound_ref):
    row, grp = pl.program_id(0), pl.program_id(1)

    @pl.when(grp == 0)
    def _():
        x = x_ref[...]
        u = dot(x, a_ref[...]).astype(BF)
        u_ref[...] = u
        for i in range(3):
            acc = dot(x, w_ref[WIDTH * i:WIDTH * (i + 1), :])
            if i != 1:
                acc += dot(u, b_ref[i // 2])
            qkv_ref[:, WIDTH * i:WIDTH * (i + 1)] = acc.astype(BF)
        key = lax.broadcasted_iota(jnp.int32, (SEQ, 128), 0)
        bound_ref[...] = jnp.where(key < len_ref[row], 3.0e38, -8.0e9)

    lane = lax.broadcasted_iota(jnp.int32, (SEQ, 128), 1)
    low = lane < HEAD_DIM
    bound = bound_ref[...]
    bound = jnp.concatenate([bound] * 4, axis=1)
    for pair in range(GROUP // 2):
        at = pl.multiple_of(grp * (GROUP * HEAD_DIM) + pair * 128, 128)
        q = qkv_ref[:, pl.ds(at, 128)]
        k = qkv_ref[:, pl.ds(WIDTH + at, 128)]
        v = qkv_ref[:, pl.ds(2 * WIDTH + at, 128)]
        outs = []
        for half in range(2):
            mine = low if half == 0 else ~low
            qh = jnp.where(mine, q, jnp.zeros_like(q))
            vh = jnp.where(mine, v, jnp.ones_like(v))
            s = jnp.minimum(dot_nt(k, qh), bound)
            top = jnp.max(s, axis=0, keepdims=True)
            e = jnp.exp2((s - top) * EXP2_SCALE).astype(BF)
            e_ref[0, pair * 2 + half] = e
            ot = dot_tn(vh, e)
            if half == 0:
                o_t, l = ot[:HEAD_DIM], ot[HEAD_DIM:HEAD_DIM + 8]
            else:
                o_t, l = ot[HEAD_DIM:], ot[0:8]
            r = 1.0 / l
            rinv_ref[0, grp * GROUP + pair * 2 + half] = r
            outs.append(o_t * r[0:1])
        both = jnp.concatenate(outs, axis=0)
        o_ref[:, pl.ds(at, 128)] = both.T.astype(BF)

    @pl.when(grp == pl.num_programs(1) - 1)
    def _():
        h = x_ref[...].astype(F32) + dot(o_ref[...], w_ref[3 * WIDTH:, :])
        c = h - mean_rows(h)
        r = lax.rsqrt(mean_rows(c * c) + EPS)
        n1_ref[...] = (c * r * g_ref[...]).astype(BF)
        r1_ref[...] = jnp.broadcast_to(r, (SEQ, 128))


def attend_forward(lengths, x, w, a, b, g):
    rows = lengths.shape[0]
    tokens = rows * SEQ
    steps = HEADS // GROUP
    row_block = lambda width: pl.BlockSpec((SEQ, width), lambda r, s: (r, 0))
    whole = lambda *shape: pl.BlockSpec(shape, lambda r, s: (0,) * len(shape), pipeline_mode=pl.Buffered(1))
    return pl.pallas_call(
        attend_kernel,
        grid=(rows, steps),
        in_specs=[
            pl.BlockSpec(memory_space=pltpu.SMEM),
            row_block(WIDTH), whole(4 * WIDTH, WIDTH), whole(WIDTH, 2 * RANK),
            whole(2, 2 * RANK, WIDTH), whole(1, WIDTH),
        ],
        out_specs=[
            row_block(3 * WIDTH), row_block(2 * RANK), row_block(WIDTH),
            pl.BlockSpec((1, GROUP, SEQ, SEQ), lambda r, s: (r, s, 0, 0)),
            pl.BlockSpec((1, HEADS, 8, SEQ), lambda r, s: (r, 0, 0, 0)),
            row_block(WIDTH), row_block(128),
        ],
        out_shape=[
            jax.ShapeDtypeStruct((tokens, 3 * WIDTH), BF),
            jax.ShapeDtypeStruct((tokens, 2 * RANK), BF),
            jax.ShapeDtypeStruct((tokens, WIDTH), BF),
            jax.ShapeDtypeStruct((rows, HEADS, SEQ, SEQ), BF),
            jax.ShapeDtypeStruct((rows, HEADS, 8, SEQ), F32),
            jax.ShapeDtypeStruct((tokens, WIDTH), BF),
            jax.ShapeDtypeStruct((tokens, 128), F32),
        ],
        scratch_shapes=[pltpu.VMEM((SEQ, 128), F32)],
        compiler_params=params(2),
        name="attend_forward",
    )(lengths, x, w, a, b, g)


BLOCK = 256
CHUNK = 768


def normal_parts(z):
    d = jnp.exp2(z * z * (-0.5 * 1.4426950408889634))
    t = 1.0 / (1.0 + jnp.abs(z) * (0.3275911 * 0.7071067811865476))
    q = t * (0.5 * 0.254829592 + t * (0.5 * -0.284496736 + t * (0.5 * 1.421413741
             + t * (0.5 * -1.453152027 + t * (0.5 * 1.061405429)))))
    tail = q * d
    cdf = jnp.where(z < 0, tail, 1.0 - tail)
    return cdf, d * 0.3989422804014327


def ffn_kernel(n1_ref, w1_ref, w2_ref, g_ref, gd_ref, x2_ref, r2_ref):
    n1 = n1_ref[...]
    f = n1.astype(F32)
    for j in range(4):
        z = dot(n1, w1_ref[j])
        cdf, pdf = normal_parts(z)
        gd_ref[:, CHUNK * j:CHUNK * (j + 1)] = (cdf + z * pdf).astype(BF)
        f = f + dot((z * cdf).astype(BF), w2_ref[j])
    c = f - mean_rows(f)
    r = lax.rsqrt(mean_rows(c * c) + EPS)
    x2_ref[...] = (c * r * g_ref[...]).astype(BF)
    r2_ref[...] = jnp.broadcast_to(r, (BLOCK, 128))


def ffn_forward(n1, w1, w2, g):
    tokens = n1.shape[0]
    block = lambda width: pl.BlockSpec((BLOCK, width), lambda s: (s, 0))
    whole = lambda *shape: pl.BlockSpec(shape, lambda s: (0,) * len(shape), pipeline_mode=pl.Buffered(1))
    return pl.pallas_call(
        ffn_kernel,
        grid=(tokens // BLOCK,),
        in_specs=[block(WIDTH), whole(4, WIDTH, CHUNK), whole(4, CHUNK, WIDTH), whole(1, WIDTH)],
        out_specs=[block(4 * CHUNK), block(WIDTH), block(128)],
        out_shape=[
            jax.ShapeDtypeStruct((tokens, 4 * CHUNK), BF),
            jax.ShapeDtypeStruct((tokens, WIDTH), BF),
            jax.ShapeDtypeStruct((tokens, 128), F32),
        ],
        compiler_params=params(1),
        name="ffn_forward",
    )(n1, w1, w2, g)


def norm_back(e, m, r):
    return r * (e - mean_rows(e) - m * mean_rows(e * m))


def ffn_back_kernel(dy_ref, x2_ref, r2_ref, n1_ref, r1_ref, gd_ref, w1_ref, w2_ref, wo_ref,
                    g1_ref, g2_ref, dh_ref, do_ref):
    g2, g1 = g2_ref[...], g1_ref[...]
    dh2 = norm_back(dy_ref[...].astype(F32) * g2, x2_ref[...].astype(F32) * (1.0 / g2), r2_ref[:, 0:1])
    df = dh2.astype(BF)
    dn = dh2
    for j in range(4):
        dz = (dot_nt(df, w2_ref[j]) * gd_ref[:, CHUNK * j:CHUNK * (j + 1)].astype(F32)).astype(BF)
        dn = dn + dot_nt(dz, w1_ref[j])
    dh = norm_back(dn * g1, n1_ref[...].astype(F32) * (1.0 / g1), r1_ref[:, 0:1])
    dh_ref[...] = dh
    do_ref[...] = dot_nt(dh.astype(BF), wo_ref[...]).astype(BF)


def ffn_backward(dy, x2, r2, n1, r1, gd, w1, w2, w, g1, g2):
    tokens = n1.shape[0]
    block = lambda width: pl.BlockSpec((BLOCK, width), lambda s: (s, 0))
    whole = lambda *shape: pl.BlockSpec(shape, lambda s: (0,) * len(shape), pipeline_mode=pl.Buffered(1))
    return pl.pallas_call(
        ffn_back_kernel,
        grid=(tokens // BLOCK,),
        in_specs=[block(WIDTH), block(WIDTH), block(128), block(WIDTH), block(128), block(4 * CHUNK),
                  whole(4, WIDTH, CHUNK), whole(4, CHUNK, WIDTH),
                  pl.BlockSpec((WIDTH, WIDTH), lambda s: (3, 0), pipeline_mode=pl.Buffered(1)),
                  whole(1, WIDTH), whole(1, WIDTH)],
        out_specs=[block(WIDTH), block(WIDTH)],
        out_shape=[jax.ShapeDtypeStruct((tokens, WIDTH), F32), jax.ShapeDtypeStruct((tokens, WIDTH), BF)],
        compiler_params=params(1),
        name="ffn_backward",
    )(dy, x2, r2, n1, r1, gd, w1, w2, w, g1, g2)


def attend_back_kernel(do_ref, dh_ref, x_ref, u_ref, qkv_ref, o_ref, e_ref, rinv_ref, w_ref, a_ref, b_ref,
                       dx_ref, ga_ref, gb_ref, d_ref):
    row, grp = pl.program_id(0), pl.program_id(1)
    lane = lax.broadcasted_iota(jnp.int32, (SEQ, 128), 1)
    low = lane < HEAD_DIM
    for pair in range(GROUP // 2):
        at = pl.multiple_of(grp * (GROUP * HEAD_DIM) + pair * 128, 128)
        q = qkv_ref[:, pl.ds(at, 128)]
        k = qkv_ref[:, pl.ds(WIDTH + at, 128)]
        v = qkv_ref[:, pl.ds(2 * WIDTH + at, 128)]
        head = grp * GROUP + pair * 2
        scale = jnp.concatenate([rinv_ref[0, head]] * 8 + [rinv_ref[0, head + 1]] * 8, axis=0).T
        dos = do_ref[:, pl.ds(at, 128)].astype(F32) * scale
        other = pltpu.roll(-dos * o_ref[:, pl.ds(at, 128)].astype(F32), HEAD_DIM, 1).astype(BF)
        dos = dos.astype(BF)
        dvs, dks, dqs = [], [], []
        for half in range(2):
            mine = low if half == 0 else ~low
            e = e_ref[0, pair * 2 + half]
            dp = dot_nt(jnp.where(mine, v, jnp.ones_like(v)), jnp.where(mine, dos, other))
            ds = (dp * e.astype(F32)).astype(BF)
            dvs.append(dot(e, dos))
            dks.append(dot(ds, q))
            dqs.append(dot_tn(k, ds)[half * HEAD_DIM:(half + 1) * HEAD_DIM])
        d_ref[:, pl.ds(2 * WIDTH + at, 128)] = jnp.where(low, dvs[0], dvs[1]).astype(BF)
        d_ref[:, pl.ds(WIDTH + at, 128)] = (jnp.where(low, dks[0], dks[1]) * HEAD_DIM ** (-0.5)).astype(BF)
        d_ref[:, pl.ds(at, 128)] = (jnp.concatenate(dqs, axis=0) * HEAD_DIM ** (-0.5)).T.astype(BF)

    @pl.when((row == 0) & (grp == 0))
    def _():
        ga_ref[...] = jnp.zeros_like(ga_ref)
        gb_ref[...] = jnp.zeros_like(gb_ref)

    @pl.when(grp == pl.num_programs(1) - 1)
    def _():
        dq, dk, dv = (d_ref[:, WIDTH * i:WIDTH * (i + 1)] for i in range(3))
        du = (dot_nt(dq, b_ref[0]) + dot_nt(dv, b_ref[1])).astype(BF)
        ga_ref[...] += dot_tn(du, x_ref[...])
        u = u_ref[...]
        u2 = u + u
        gb_ref[0] += dot_tn(u2, dq)
        gb_ref[1] += dot_tn(u2, dv)
        dx_ref[...] = (dh_ref[...] + dot_nt(dq, w_ref[0:WIDTH]) + dot_nt(dk, w_ref[WIDTH:2 * WIDTH])
                       + dot_nt(dv, w_ref[2 * WIDTH:3 * WIDTH]) + dot_nt(du, a_ref[...]))


def attend_backward(do, dh, x, u, qkv, o, e, rinv, w, a, b):
    rows = e.shape[0]
    tokens = rows * SEQ
    row_block = lambda width: pl.BlockSpec((SEQ, width), lambda r, s: (r, 0))
    whole = lambda *shape: pl.BlockSpec(shape, lambda r, s: (0,) * len(shape), pipeline_mode=pl.Buffered(1))
    return pl.pallas_call(
        attend_back_kernel,
        grid=(rows, HEADS // GROUP),
        in_specs=[
            row_block(WIDTH), row_block(WIDTH), row_block(WIDTH), row_block(2 * RANK), row_block(3 * WIDTH),
            row_block(WIDTH),
            pl.BlockSpec((1, GROUP, SEQ, SEQ), lambda r, s: (r, s, 0, 0)),
            pl.BlockSpec((1, HEADS, 8, SEQ), lambda r, s: (r, 0, 0, 0)),
            whole(3 * WIDTH, WIDTH), whole(WIDTH, 2 * RANK), whole(2, 2 * RANK, WIDTH),
        ],
        out_specs=[
            row_block(WIDTH),
            pl.BlockSpec((2 * RANK, WIDTH), lambda r, s: (0, 0)),
            pl.BlockSpec((2, 2 * RANK, WIDTH), lambda r, s: (0, 0, 0)),
        ],
        out_shape=[
            jax.ShapeDtypeStruct((tokens, WIDTH), F32),
            jax.ShapeDtypeStruct((2 * RANK, WIDTH), F32),
            jax.ShapeDtypeStruct((2, 2 * RANK, WIDTH), F32),
        ],
        scratch_shapes=[pltpu.VMEM((SEQ, 3 * WIDTH), BF)],
        compiler_params=params(2),
        name="attend_backward",
    )(do, dh, x, u, qkv, o, e, rinv, w, a, b)


def local(axes, tokens, lengths, attention, down, up, expand, project, gains, cotangent):
    layers = attention.shape[0]
    weights = []
    for l in range(layers):
        w = lax.all_gather(attention[l], axes, axis=0, tiled=True)
        w1 = lax.all_gather(expand[l], axes[1], axis=0)
        w2 = lax.all_gather(project[l], axes[1], axis=0)
        if w1.shape[0] != 4:
            w1 = w1.transpose(1, 0, 2).reshape(WIDTH, 4, CHUNK).transpose(1, 0, 2)
            w2 = w2.reshape(4, CHUNK, WIDTH)
        a = jnp.concatenate([down[l, 0], down[l, 1]], axis=1)
        twice = up[l] + up[l]
        zero = jnp.zeros_like(up[l, 0])
        b = jnp.stack([jnp.concatenate([twice[0], zero], axis=0), jnp.concatenate([zero, twice[1]], axis=0)])
        weights.append((w, w1, w2, a, b, gains[l, 0:1], gains[l, 1:2]))
    x = tokens
    saved = []
    for l in range(layers):
        w, w1, w2, a, b, g1, g2 = weights[l]
        qkv, u, o, e, rinv, n1, r1 = attend_forward(lengths, x, w, a, b, g1)
        gd, x2, r2 = ffn_forward(n1, w1, w2, g2)
        saved.append((x, qkv, u, o, e, rinv, n1, r1, gd, x2, r2))
        x = x2
    dy = cotangent
    grads = [None] * layers
    for l in reversed(range(layers)):
        w, w1, w2, a, b, g1, g2 = weights[l]
        x_in, qkv, u, o, e, rinv, n1, r1, gd, x2, r2 = saved[l]
        dh, do = ffn_backward(dy, x2, r2, n1, r1, gd, w1, w2, w, g1, g2)
        dy, ga, gb = attend_backward(do, dh, x_in, u, qkv, o, e, rinv, w, a, b)
        grads[l] = jnp.concatenate([ga, gb[0, :RANK], gb[1, RANK:]], axis=0)
    total = lax.psum(jnp.stack(grads), axes)
    a_grad = total[:, :2 * RANK].reshape(layers, 2, RANK, WIDTH).transpose(0, 1, 3, 2)
    b_grad = total[:, 2 * RANK:].reshape(layers, 2, RANK, WIDTH)
    return x, dy, a_grad, b_grad


def solution(mesh):
    axes = tuple(mesh.axis_names)
    dp, tensor = axes
    placed = (
        P(axes, None), P(axes), P(None, axes, None), P(), P(),
        P(None, None, tensor), P(None, tensor, None), P(), P(axes, None),
    )
    return jax.shard_map(
        functools.partial(local, axes),
        mesh=mesh,
        in_specs=placed,
        out_specs=(P(axes, None), P(axes, None), P(), P()),
        check_vma=False,
    )
```

time: 769 us -> 552 us (0.72)
  matrix products: 378 us -> 0 us
  Pallas kernels: 0 us -> 199 us
  waiting for transfers between devices: 198 us -> 325 us
  local copies, waits for them, and re-layouts: 107 us -> 11.3 us
  other arithmetic: 60.7 us -> 2.77 us
    dot_general x74 -> x0, matrix products: 378 us -> none  [the longest x20 142 us: matrix_product(): return jnp.dot(left_side, right_side, preferred_element_type=jnp.float32)]
    pallas_call x0 -> x8, Pallas kernels: none -> 199 us  [the longest x2 56.9 us: attend_forward(): pl.pallas_call(attend_kernel, grid=(rows, steps), in_specs=[pl.BlockSpec(...]
    all_gather x6, waiting for transfers between devices: 87.9 us -> 200 us  [the longest x2 102 us: local(): w = lax.all_gather(attention[l], axes, axis=0, tiled=True)]
    convert_element_type x5 -> x0, other arithmetic: 28.8 us -> none  [the longest x4 28.4 us: attend_back(): grad_scores = (row_probs * (grad_probs - jnp.sum(grad_probs * row_probs,...]
    dynamic_slice x36 -> x0, local copies, waits for them, and re-layouts: 27.4 us -> none  [local(): lax.map(attend_row, (query_rows.reshape(local_rows, SEQ, MODEL_WIDTH), ke...]
    reduce_sum x12 -> x0, other arithmetic: 25.4 us -> none  [the longest x4 11.1 us: layer_norm(): centred = values - centre]
    while x70 -> x0, local copies, waits for them, and re-layouts: 24 us -> none  [the longest x6 13.9 us: local(): lax.map(attend_row, (query_rows.reshape(local_rows, SEQ, MODEL_WIDTH), ke...]
    unnamed x154 -> x12, local copies, waits for them, and re-layouts: 19.7 us -> 0.03 us
  transfers between devices with their start and end apart: 7 -> 7, of which waited for: 3 -> 7; matrix products, arithmetic and copies ran while one was open for 29% -> 2% of each run, Pallas kernels for 0% -> 14%
where the time goes in v1:
time: 552 us
  waiting for transfers between devices  325 us (59%)
  Pallas kernels  199 us (36%)
  between operations  14.3 us (3%)
  local copies, waits for them, and re-layouts  11.3 us (2%)
    psum x1, waiting for transfers between devices, local(): total = lax.psum(jnp.stack(grads), axes)  123 us
    all_gather x2, waiting for transfers between devices, local(): w = lax.all_gather(attention[l], axes, axis=0, tiled=True)  102 us
    all_gather x2, waiting for transfers between devices, local(): w2 = lax.all_gather(project[l], axes[1], axis=0)  77.9 us
    pallas_call x2, Pallas kernels, attend_forward(): pl.pallas_call(attend_kernel, grid=(rows, steps), in_specs=[pl.BlockSpec(...  56.9 us
    pallas_call x2, Pallas kernels, attend_backward(): pl.pallas_call(attend_back_kernel, grid=(rows, HEADS // GROUP), in_specs=...  56.5 us
    pallas_call x2, Pallas kernels, ffn_forward(): pl.pallas_call(ffn_kernel, grid=(tokens // BLOCK,), in_specs=[block(WIDTH...  44.2 us
    pallas_call x2, Pallas kernels, ffn_backward(): pl.pallas_call(ffn_back_kernel, grid=(tokens // BLOCK,), in_specs=[block(...  41 us
    all_gather x2, waiting for transfers between devices, local(): w1 = lax.all_gather(expand[l], axes[1], axis=0)  19.9 us
  transfers between devices with their start and end apart: 7, of which 7 were waited for; matrix products, arithmetic and copies ran while one was open for 2% of the time, Pallas kernels for 14%

profile of v1, /device:TPU:0, one launch (start us, length us, event | category | flops | bytes accessed | tf_op | source)
XLA Modules:
  0.0 551.9 jit_solution(9775055074142318858)
XLA Ops:
  7.2 1.7 fusion.2
  9.0 0.0 all-gather.9.cloned.1.call-start
  9.0 3.3 fusion.1
  12.4 0.0 all-gather.11.cloned.1.call-start
  12.4 1.6 fusion
  14.1 0.5 all-gather.19.cloned.1.call-update
  14.7 0.5 all-gather.13.cloned.1.call-update
  15.3 0.5 all-gather.15.cloned.1.call-update
  15.9 0.8 copy.17.a_ref
  16.7 0.8 copy.18.a_ref
  17.6 0.6 pad_maximum_fusion.2.b_ref
  18.2 0.6 pad_maximum_fusion.1.b_ref
  18.8 0.6 slice_bitcast_fusion.14
  19.5 57.8 %all-gather.17.cloned.1.call-done = bf16[1,3072,768]{2,1,0:T(8,128)(2,1)} async-done(((bf16[1,96,768]{2,1,0:T(8,128)(2,1)}), bf16[1,3072,768]{2,1,0:T(8,128)(2,1)}) %all-gather.17.cloned.1.call-update) | async-done | bytes 4718608 | tf_op jit(solution)/shard_map/all_gather | solution.py:300
  77.2 28.4 %attend_forward.2 = (bf16[1024,2304]{1,0:T(8,128)(2,1)}, bf16[1024,16]{1,0:T(8,128)(2,1)}, bf16[1024,768]{1,0:T(8,128)(2,1)}, bf16[2,12,512,512]{3,2,1,0:T(8,128...) custom-call(s32[2]{0:T(128)} %len_ref.3, bf16[1024,768]{1,0:T(8,128)(2,1)} %x_ref.3, ...), custom_call_target="tpu_custom_call" | custom-call | tf_op jit(solution)/shard_map/attend_forward/pallas_call | solution.py:107
  105.6 10.0 %all-gather.9.cloned.1.call-done.w1_ref = bf16[4,768,768]{2,1,0:T(8,128)(2,1)} async-done(((bf16[1,768,768]{2,1,0:T(8,128)(2,1)}), bf16[4,768,768]{2,1,0:T(8,128)(2,1)}) %all-gather.9.cloned.1.call-update) | async-done | bytes 4718608 | tf_op jit(solution)/shard_map/all_gather | solution.py:301
  115.7 39.1 %all-gather.11.cloned.1.call-done.w2_ref = bf16[4,768,768]{2,1,0:T(8,128)(2,1)} async-done(((bf16[1,768,768]{2,1,0:T(8,128)(2,1)}), bf16[4,768,768]{2,1,0:T(8,128)(2,1)}) %all-gather.11.cloned.1.call-update) | async-done | bytes 4718608 | tf_op jit(solution)/shard_map/all_gather | solution.py:302
  154.7 22.1 %ffn_forward.2 = (bf16[1024,3072]{1,0:T(8,128)(2,1)}, bf16[1024,768]{1,0:T(8,128)(2,1)}, f32[1024,128]{1,0:T(8,128)}) custom-call(bf16[1024,768]{1,0:T(8,128)(2,1)} %get-tuple-element.34.n1_ref, bf16[4,768,768]{2,1,0:T(8,128)(2,1)} %all-gather.9.cloned.1.call-done.w1_ref, bf16[4,768,768]{2,1,0:T(8,128)(2,1)} %all-gather.11.cloned.1.call-done.w2_ref, ...), custom_call_target="tpu_custom_call" | custom-call | tf_op jit(solution)/shard_map/ffn_forward/pallas_call | solution.py:168
  176.8 44.3 %all-gather.19.cloned.1.call-done = bf16[1,3072,768]{2,1,0:T(8,128)(2,1)} async-done(((bf16[1,96,768]{2,1,0:T(8,128)(2,1)}), bf16[1,3072,768]{2,1,0:T(8,128)(2,1)}) %all-gather.19.cloned.1.call-update) | async-done | bytes 4718608 | tf_op jit(solution)/shard_map/all_gather | solution.py:300
  221.1 28.5 %attend_forward.3 = (bf16[1024,2304]{1,0:T(8,128)(2,1)}, bf16[1024,16]{1,0:T(8,128)(2,1)}, bf16[1024,768]{1,0:T(8,128)(2,1)}, bf16[2,12,512,512]{3,2,1,0:T(8,128...) custom-call(s32[2]{0:T(128)} %len_ref.3, ...), custom_call_target="tpu_custom_call" | custom-call | tf_op jit(solution)/shard_map/attend_forward/pallas_call | solution.py:107
  249.6 9.8 %all-gather.13.cloned.1.call-done.w1_ref = bf16[4,768,768]{2,1,0:T(8,128)(2,1)} async-done(((bf16[1,768,768]{2,1,0:T(8,128)(2,1)}), bf16[4,768,768]{2,1,0:T(8,128)(2,1)}) %all-gather.13.cloned.1.call-update) | async-done | bytes 4718608 | tf_op jit(solution)/shard_map/all_gather | solution.py:301
  259.5 38.8 %all-gather.15.cloned.1.call-done.w2_ref = bf16[4,768,768]{2,1,0:T(8,128)(2,1)} async-done(((bf16[1,768,768]{2,1,0:T(8,128)(2,1)}), bf16[4,768,768]{2,1,0:T(8,128)(2,1)}) %all-gather.15.cloned.1.call-update) | async-done | bytes 4718608 | tf_op jit(solution)/shard_map/all_gather | solution.py:302
  298.3 22.1 %ffn_forward.3 = (bf16[1024,3072]{1,0:T(8,128)(2,1)}, bf16[1024,768]{1,0:T(8,128)(2,1)}, f32[1024,128]{1,0:T(8,128)}) custom-call(bf16[1024,768]{1,0:T(8,128)(2,1)} %get-tuple-element.36.n1_ref, bf16[4,768,768]{2,1,0:T(8,128)(2,1)} %all-gather.13.cloned.1.call-done.w1_ref, bf16[4,768,768]{2,1,0:T(8,128)(2,1)} %all-gather.15.cloned.1.call-done.w2_ref, ...), custom_call_target="tpu_custom_call" | custom-call | tf_op jit(solution)/shard_map/ffn_forward/pallas_call | solution.py:168
  320.4 20.6 %ffn_backward.2 = (f32[1024,768]{1,0:T(8,128)}, bf16[1024,768]{1,0:T(8,128)(2,1)}) custom-call(bf16[1024,768]{1,0:T(8,128)(2,1)} %dy_ref.1, bf16[1024,768]{1,0:T(8,128)(2,1)} %get-tuple-element.30.x2_ref, f32[1024,128]{1,0:T(8,128)} %get-tuple-element.38.r2_ref, bf16[1024,768]{1,0:T(8,128)(2,1)} %get-tuple-element.36.n1_ref, ...), custom_call_target="tpu_custom_call" | custom-call | tf_op jit(solution)/shard_map/ffn_backward/pallas_call | solution.py:205
  340.9 28.1 %attend_backward.2 = (f32[1024,768]{1,0:T(8,128)}, f32[16,768]{1,0:T(8,128)}, f32[2,16,768]{2,1,0:T(8,128)}) custom-call(bf16[1024,768]{1,0:T(8,128)(2,1)} %get-tuple-element.41.do_ref, f32[1024,768]{1,0:T(8,128)} %get-tuple-element.42.dh_ref, bf16[1024,768]{1,0:T(8,128)(2,1)} %get-tuple-element.35.x_ref.x2_ref, bf16[1024,16]{1,0:T(8,128)(2,1)} %get-tuple-element.43.u_ref, ...), custom_call_target="tpu_custom_call" | custom-call | tf_op jit(solution)/shard_map/attend_backward/pallas_call | solution.py:270
  369.0 20.5 %ffn_backward.3 = (f32[1024,768]{1,0:T(8,128)}, bf16[1024,768]{1,0:T(8,128)(2,1)}) custom-call(f32[1024,768]{1,0:T(8,128)} %get-tuple-element.48.dy_ref, bf16[1024,768]{1,0:T(8,128)(2,1)} %get-tuple-element.35.x_ref.x2_ref, f32[1024,128]{1,0:T(8,128)} %get-tuple-element.49.r2_ref, bf16[1024,768]{1,0:T(8,128)(2,1)} %get-tuple-element.34.n1_ref, ...), custom_call_target="tpu_custom_call" | custom-call | tf_op jit(solution)/shard_map/ffn_backward/pallas_call | solution.py:205
  389.5 28.4 %attend_backward.3 = (f32[1024,768]{1,0:T(8,128)}, f32[16,768]{1,0:T(8,128)}, f32[2,16,768]{2,1,0:T(8,128)}) custom-call(bf16[1024,768]{1,0:T(8,128)(2,1)} %get-tuple-element.52.do_ref, f32[1024,768]{1,0:T(8,128)} %get-tuple-element.53.dh_ref, bf16[1024,768]{1,0:T(8,128)(2,1)} %x_ref.3, bf16[1024,16]{1,0:T(8,128)(2,1)} %get-tuple-element.54.u_ref, ...), custom_call_target="tpu_custom_call" | custom-call | tf_op jit(solution)/shard_map/attend_backward/pallas_call | solution.py:270
  417.9 0.8 slice_bitcast_fusion.5
  418.7 0.8 maximum_bitcast_fusion
  419.5 0.7 pad_maximum_fusion
  420.3 123.2 %all-reduce.6.cloned.1.call-done = f32[2,32,768]{2,1,0:T(8,128)} async-done(((f32[2,32,768]{2,1,0:T(8,128)}), f32[2,32,768]{2,1,0:T(8,128)}) %all-reduce.6.cloned.1.call-update) | async-done | bytes 196624 | tf_op jit(solution)/shard_map/psum | solution.py:327
  543.4 1.6 slice_bitcast_fusion
  (32 shorter events, 0.3 us)
Async XLA Ops:
  7.2 70.1 %all-gather.17.cloned.1.call-start = ((), (), s32[]{:S(2)}) async-start(), calls=%async_computation.5 | async-start | bytes 4866048 | tf_op jit(solution)/shard_map/all_gather | solution.py:300
  9.0 3.5 copy-start
  9.0 106.7 %all-gather.9.cloned.1.call-start = ((), (), s32[]{:S(2)}) async-start(), calls=%async_computation | async-start | bytes 5898240 | tf_op jit(solution)/shard_map/all_gather | solution.py:301
  12.4 142.3 %all-gather.11.cloned.1.call-start = ((), (), s32[]{:S(2)}) async-start(), calls=%async_computation.1 | async-start | bytes 5898240 | tf_op jit(solution)/shard_map/all_gather | solution.py:302
  14.0 1.8 copy-start.1
  14.0 3.5 copy-start.2
  14.0 4.8 copy-start.5
  14.1 207.0 %all-gather.19.cloned.1.call-start = ((), (), s32[]{:S(2)}) async-start(), calls=%async_computation.6 | async-start | bytes 4866048 | tf_op jit(solution)/shard_map/all_gather | solution.py:300
  14.6 244.8 %all-gather.13.cloned.1.call-start = ((), (), s32[]{:S(2)}) async-start(), calls=%async_computation.2 | async-start | bytes 5898240 | tf_op jit(solution)/shard_map/all_gather | solution.py:301
  15.2 283.1 %all-gather.15.cloned.1.call-start = ((), (), s32[]{:S(2)}) async-start(), calls=%async_computation.3 | async-start | bytes 5898240 | tf_op jit(solution)/shard_map/all_gather | solution.py:302
  15.8 527.6 %all-reduce.6.cloned.1.call-start = ((), (), s32[]{:S(2)}) async-start(), calls=%async_computation.4 | async-start | bytes 393216 | tf_op jit(solution)/shard_map/psum | solution.py:327
  389.5 29.2 %copy-start.4 = (f32[2,16,768]{2,1,0:T(8,128)S(1)}, f32[2,16,768]{2,1,0:T(8,128)}, u32[]{:S(2)}) copy-start(f32[2,16,768]{2,1,0:T(8,128)} %get-tuple-element.63) | copy-start | bytes 294916
  389.5 30.0 %copy-start.3 = (f32[16,768]{1,0:T(8,128)S(1)}, f32[16,768]{1,0:T(8,128)}, u32[]{:S(2)}) copy-start(f32[16,768]{1,0:T(8,128)} %get-tuple-element.62) | copy-start | bytes 147460
Sparse Core Ops, SparseCore 0:
  10.9 66.2 all-gather.16
  79.4 36.2 all-gather.8
  117.2 37.4 all-gather.10
  157.5 63.5 all-gather.18
  223.1 36.3 all-gather.12
  260.9 37.3 all-gather.14
  420.4 122.9 all-reduce.5
